TPU v7x, 512 devices: a whole 4x8x8 slice. The times are simulated.
512 devices in a mesh: sample: 8 (over z_lo, core), slab: 64 (over z_hi, x, y).
Axes of the slice: x: 4, y: 8, z: 8 (z_hi: 2, z_lo: 4; z = z_hi * 4 + z_lo), core: 2. Of those that a mesh axis runs over, the one named last changes fastest.
Arguments:
- deviation: bfloat16 [8, 19, 256, 64, 128], P('sample', None, 'slab'), may hold values from -3 to 3
- solid: int32 [8, 256, 64, 128], P('sample', 'slab'), may hold values from 0 to 1, as said below
- region: int32 [8, 256, 64, 128], P('sample', 'slab'), may hold values from 0 to 1023
Outputs:
- populations: float32 [8, 19, 256, 64, 128], P('sample', None, 'slab')
- cdf: float32 [64, 1024, 64], P('slab', 'sample')
Inputs may be any that keep to these rules, and one draw needn't show every extreme that they name: `solid`: the share of rock voxels differs from z-plane to z-plane.
All inputs are finite; a program needn't handle non-finite values.
Results may differ from a plain program's by a relative error of at most 0.0003.
Values sent between devices are 32-bit elements; how exact they have to be, the bound alone decides.
No kernel may reach another device: no remote copies, remote signals or barrier semaphores. Data moves between devices by JAX's collectives and lax.ppermute only.
A program may use at most 64 MiB of HBM per device.

v0:
```python
import functools

import jax
import jax.numpy as jnp
from jax import lax
from jax.experimental import pallas as pl
from jax.experimental.pallas import tpu as pltpu
from jax.sharding import PartitionSpec as P

LEVELS = 64
AMPLITUDE = 0.3
SPEED_TOP = 0.12
MOVES = [
    (0, 0, 0),
    (1, 0, 0),
    (-1, 0, 0),
    (0, 1, 0),
    (0, -1, 0),
    (0, 0, 1),
    (0, 0, -1),
    (1, 1, 0),
    (-1, -1, 0),
    (1, -1, 0),
    (-1, 1, 0),
    (1, 0, 1),
    (-1, 0, -1),
    (1, 0, -1),
    (-1, 0, 1),
    (0, 1, 1),
    (0, -1, -1),
    (0, 1, -1),
    (0, -1, 1),
]
OPPOSITE = [0, 2, 1, 4, 3, 6, 5, 8, 7, 10, 9, 12, 11, 14, 13, 16, 15, 18, 17]
WEIGHTS = [1.0 / 3.0] + [1.0 / 18.0] * 6 + [1.0 / 36.0] * 12
FLAT = [q for q in range(19) if MOVES[q][2] == 0]
UP = [q for q in range(19) if MOVES[q][2] == 1]
DOWN = [q for q in range(19) if MOVES[q][2] == -1]
FLAT_RUNS = ((0, 5), (7, 4))
NX, NY, CZ = 128, 64, 4
STEP = 8
VMEM_BYTES = 48 * 1024 * 1024
BF16 = jnp.bfloat16
F32 = jnp.float32


def collide(f, rock):
    sx, sy, sz = f[1] + f[2], f[3] + f[4], f[5] + f[6]
    s7, s9, s11 = f[7] + f[8], f[9] + f[10], f[11] + f[12]
    s13, s15, s17 = f[13] + f[14], f[15] + f[16], f[17] + f[18]
    dx, dy, dz = f[1] - f[2], f[3] - f[4], f[5] - f[6]
    d7, d9, d11 = f[7] - f[8], f[9] - f[10], f[11] - f[12]
    d13, d15, d17 = f[13] - f[14], f[15] - f[16], f[17] - f[18]
    sxy, sxz, syz = s7 + s9, s11 + s13, s15 + s17
    one, two = sx + (sy + sz), sxy + (sxz + syz)
    rho = f[0] + one + two
    ax, bx = d7 + d9, d11 + d13
    ay, by = d15 + d17, d7 - d9
    az, bz = d11 - d13, d15 - d17
    jx, jy, jz = dx + (ax + bx), dy + (ay + by), dz + (az + bz)
    inv = 1.0 / rho
    ux, uy, uz = jx * inv, jy * inv, jz * inv
    xx, yy, zz = jx * ux, jy * uy, jz * uz
    square = xx + yy + zz
    e = (1.19 * 19 / 2394) * (two - f[0] - square)
    eps = (1.4 / 252) * (9.0 * f[0] - 7.0 * one - 2.0 * two + 5.5 * square)
    even0 = 12.0 * eps - 30.0 * e
    base1 = -11.0 * e - 4.0 * eps
    base2 = 8.0 * e + eps
    p1, p2, px = 3.0 * sx - one, two - 3.0 * syz, 3.0 * xx - square
    pxx = (1.25 / 36) * (p1 + p2 - px)
    pixx = (1.4 / 72) * (p2 - 2.0 * p1 + 0.5 * px)
    w1, w2, pw = sy - sz, sxy - sxz, yy - zz
    pww = (1.25 / 12) * (w1 + w2 - pw)
    piww = (1.4 / 24) * (w2 - 2.0 * w1 + 0.5 * pw)
    pxy = (1.25 / 4) * (s7 - s9 - jx * uy)
    pxz = (1.25 / 4) * (s11 - s13 - jx * uz)
    pyz = (1.25 / 4) * (s15 - s17 - jy * uz)
    ua, va = pxx - 2.0 * pixx, pxx + pixx
    ub, vb = pww - 2.0 * piww, pww + piww
    qx = 0.05 * jx - 0.15 * dx
    qy = 0.05 * jy - 0.15 * dy
    qz = 0.05 * jz - 0.15 * dz
    mx = (1.98 / 8) * (ax - bx)
    my = (1.98 / 8) * (ay - by)
    mz = (1.98 / 8) * (az - bz)
    xp, xm, yp, ym = qx + mx, qx - mx, qy + my, qy - my
    zp, zm = qz + mz, qz - mz
    rest = base1 - ua
    xy, xz, yz = base2 + va + vb, base2 + va - vb, base2 - 2.0 * va
    pairs = {
        1: (base1 + 2.0 * ua, -4.0 * qx),
        3: (rest + ub, -4.0 * qy),
        5: (rest - ub, -4.0 * qz),
        7: (xy + pxy, xp + ym),
        9: (xy - pxy, xp - ym),
        11: (xz + pxz, xm + zp),
        13: (xz - pxz, xm - zp),
        15: (yz + pyz, yp + zm),
        17: (yz - pyz, yp - zm),
    }
    post = [jnp.where(rock, f[0], f[0] - even0)] + [None] * 18
    for q, (even, odd) in pairs.items():
        post[q] = jnp.where(rock, f[q + 1], f[q] - (even + odd))
        post[q + 1] = jnp.where(rock, f[q], f[q + 1] - (even - odd))
    return post


def put(ref, where, turn, value, q):
    cx, cy, _ = MOVES[q]
    if cx:
        value = pltpu.roll(value, cx % NX, 1)
    row = STEP * turn
    last = NY // STEP - 1
    if cy == 0:
        ref[where + (pl.ds(row, STEP),)] = value
    elif cy == 1 and turn == last:
        ref[where + (pl.ds(row + 1, STEP - 1),)] = value[: STEP - 1]
        ref[where + (pl.ds(0, 1),)] = value[STEP - 1 :]
    elif cy == -1 and turn == 0:
        ref[where + (pl.ds(0, STEP - 1),)] = value[1:]
        ref[where + (pl.ds(NY - 1, 1),)] = value[:1]
    else:
        ref[where + (pl.ds(row + cy, STEP),)] = value


def collide_plane(load, solid, dest):
    for turn in range(NY // STEP):
        f = [load(q, turn) for q in range(19)]
        post = collide(f, solid(turn) == 1)
        for q in range(19):
            if dest[q] is not None:
                ref, where = dest[q]
                put(ref, where, turn, post[q], q)


def initial(ref, where):
    def load(q, turn):
        low = turn // 2 * 16
        rows = ref[where + (q, pl.ds(low, 16))].astype(F32)
        rows = rows[(turn % 2) * 8 : (turn % 2) * 8 + 8]
        return WEIGHTS[q] + (WEIGHTS[q] * AMPLITUDE) * rows

    return load


def rows_of(ref, where):
    return lambda turn: ref[where + (pl.ds(STEP * turn, STEP),)]


class Copies:
    def __init__(self, sems):
        self.sems = sems
        self.used = 0
        self.open = []

    def start(self, source, target):
        copy = pltpu.make_async_copy(source, target, self.sems.at[self.used])
        self.used += 1
        copy.start()
        self.open.append(copy)
        return copy

    def finish(self):
        for copy in self.open:
            copy.wait()


def odd_slab():
    return lax.rem(lax.axis_index("slab"), 2)


def first_edges(dev, solid, s1, s2, flat, inner, dev_v, solid_v, s_v, flat_v, inner_v, sems_in, sems_out):
    odd = odd_slab()
    into, out = Copies(sems_in), Copies(sems_out)
    copies = []
    for side, z in ((0, 0), (1, CZ - 1)):
        copies.append(
            (into.start(solid.at[0, z], solid_v.at[side]), into.start(dev.at[0, :, z], dev_v.at[side]))
        )
    for side in range(2):
        for copy in copies[side]:
            copy.wait()
        slot = odd if side == 0 else 1 - odd
        away, home = (DOWN, UP) if side == 0 else (UP, DOWN)
        dest = [None] * 19
        for j, q in enumerate(FLAT):
            dest[q] = (flat_v, (side, j))
        for j, q in enumerate(away):
            dest[q] = (s_v, (slot, j))
        for j, q in enumerate(home):
            dest[q] = (inner_v, (side, j))
        collide_plane(initial(dev_v, (side,)), rows_of(solid_v, (side,)), dest)
        out.start(flat_v.at[side], flat.at[side])
        out.start(inner_v.at[side], inner.at[side])
    out.start(s_v.at[0], s1)
    out.start(s_v.at[1], s2)
    out.finish()


def first_inside(dev, solid, inner, edge, field, dev_v, solid_v, f_v, edge_v, g_v, sems_in, sems_out):
    into, out = Copies(sems_in), Copies(sems_out)
    into.start(solid.at[0, pl.ds(1, 2)], solid_v)
    into.start(dev.at[0, :, pl.ds(1, 2)], dev_v)
    for j, q in enumerate(UP):
        into.start(inner.at[0, j], f_v.at[0, q])
    for j, q in enumerate(DOWN):
        into.start(inner.at[1, j], f_v.at[1, q])
    into.finish()
    for side in range(2):
        dest = [None] * 19
        for q in FLAT:
            dest[q] = (f_v, (side, q))
        away, home = (DOWN, UP) if side == 0 else (UP, DOWN)
        for j, q in enumerate(away):
            dest[q] = (edge_v, (side, j))
        for q in home:
            dest[q] = (f_v, (1 - side, q))

        def load(q, turn, side=side):
            low = turn // 2 * 16
            rows = dev_v[q, side, pl.ds(low, 16)].astype(F32)
            rows = rows[(turn % 2) * 8 : (turn % 2) * 8 + 8]
            return WEIGHTS[q] + (WEIGHTS[q] * AMPLITUDE) * rows

        collide_plane(load, rows_of(solid_v, (side,)), dest)
    out.start(edge_v, edge)
    for side in range(2):
        z = side + 1
        dest = [(g_v, (q, z + MOVES[q][2])) for q in range(19)]
        collide_plane(
            lambda q, turn, side=side: f_v[side, q, pl.ds(STEP * turn, STEP)],
            rows_of(solid_v, (side,)),
            dest,
        )
    for low, count in FLAT_RUNS:
        run = pl.ds(low, count)
        out.start(g_v.at[run, pl.ds(1, 2)], field.at[0, run, pl.ds(1, 2)])
    for q in DOWN:
        out.start(g_v.at[q, pl.ds(0, 2)], field.at[0, q, pl.ds(0, 2)])
    for q in UP:
        out.start(g_v.at[q, pl.ds(2, 2)], field.at[0, q, pl.ds(2, 2)])
    out.finish()


def second_edges(solid, flat, edge, r1, r2, held, s1, s2, field, solid_v, flat_v, edge_v, r_v, s_v, g_v, sems_in, sems_out):
    del held
    odd = odd_slab()
    into, out = Copies(sems_in), Copies(sems_out)
    into.start(r1, r_v.at[0])
    into.start(r2, r_v.at[1])
    for side, z in ((0, 0), (1, CZ - 1)):
        into.start(solid.at[0, z], solid_v.at[side])
    into.start(flat, flat_v)
    into.start(edge, edge_v)
    into.finish()
    for side, z in ((0, 0), (1, CZ - 1)):
        slot = odd if side == 0 else 1 - odd
        away, home = (DOWN, UP) if side == 0 else (UP, DOWN)
        source = {}
        for j, q in enumerate(FLAT):
            source[q] = (flat_v, (side, j))
        for j, q in enumerate(away):
            source[q] = (edge_v, (side, j))
        for j, q in enumerate(home):
            source[q] = (r_v, (slot, j))
        dest = [None] * 19
        for q in FLAT:
            dest[q] = (g_v, (q, side))
        for j, q in enumerate(away):
            dest[q] = (s_v, (slot, j))
        for q in home:
            dest[q] = (g_v, (q, side))

        def load(q, turn, source=source):
            ref, where = source[q]
            return ref[where + (pl.ds(STEP * turn, STEP),)]

        collide_plane(load, rows_of(solid_v, (side,)), dest)
        for low, count in FLAT_RUNS:
            run = pl.ds(low, count)
            out.start(g_v.at[run, side], field.at[0, run, z])
        for q in home:
            out.start(g_v.at[q, side], field.at[0, q, z + MOVES[q][2]])
    out.start(s_v.at[0], s1)
    out.start(s_v.at[1], s2)
    out.finish()


def sums_of(values):
    total = [None] * 4
    for q, value in values.items():
        for axis, sign in enumerate((1,) + MOVES[q]):
            if sign:
                term = value if total[axis] is None else total[axis]
                if total[axis] is None:
                    total[axis] = value if sign > 0 else -value
                else:
                    total[axis] = term + value if sign > 0 else term - value
    return total


def level_codes(rho, jx, jy, jz, solid):
    inv = 1.0 / rho
    ux, uy, uz = jx * inv, jy * inv, jz * inv
    speed = jnp.sqrt(ux * ux + uy * uy + uz * uz)
    place = jnp.clip(speed * (LEVELS / SPEED_TOP) - 1.5, -2.0, 100.0)
    first = jnp.ceil(place)
    return jnp.where(solid == 1, 300.0, first), first - place


def add_regions(first, part, region, total, rows):
    def body(turn, carry):
        left, right = [], []
        for j in range(rows):
            row = turn * rows + j

            def spread(ref, row=row):
                return jnp.broadcast_to(ref[pl.ds(row, 1), :], (16, NX))

            a, b = spread(first).astype(BF16), spread(part).astype(BF16)
            label = spread(region)
            high = (label >> 8).astype(F32).astype(BF16)
            low = (label & 255).astype(F32).astype(BF16)
            count = lax.broadcasted_iota(jnp.int32, (16, NX), 0).astype(F32).astype(BF16)
            zero, one = jnp.zeros((16, NX), BF16), jnp.ones((16, NX), BF16)
            ramps = [
                jnp.clip((count + BF16(16 * g) - a) + b, BF16(0), BF16(1)) for g in range(LEVELS // 16)
            ]
            left.append(
                jnp.concatenate([jnp.where(high == BF16(h), r, zero) for h in range(4) for r in ramps], 0)
            )
            right.append(
                jnp.concatenate([jnp.where(low == count + BF16(16 * g), one, zero) for g in range(16)], 0)
            )
        total[...] += lax.dot_general(
            jnp.concatenate(left, 1),
            jnp.concatenate(right, 1),
            (((1,), (1,)), ((), ())),
            preferred_element_type=F32,
        )
        return carry

    lax.fori_loop(0, first.shape[0] // rows, body, 0)


def inside_regions(field, solid, region, table, part, f_v, solid_v, region_v, first_v, frac_v, table_v, part_v, sems_in, sems_out):
    into, out = Copies(sems_in), Copies(sems_out)
    for q in range(19):
        into.start(field.at[0, q], f_v.at[q])
    into.start(solid.at[0, pl.ds(1, 2)], solid_v)
    into.start(region.at[0, 1], region_v.at[pl.ds(0, NY)])
    into.start(region.at[0, 2], region_v.at[pl.ds(NY, NY)])
    into.finish()
    for side, z in ((0, 0), (1, CZ - 1)):
        have = FLAT + (DOWN if side == 0 else UP)
        for turn in range(NY // STEP):
            rows = pl.ds(STEP * turn, STEP)
            for k, value in enumerate(sums_of({q: f_v[q, z, rows] for q in have})):
                part_v[side, k, rows] = value
    out.start(part_v, part)
    for side in range(2):
        for turn in range(NY // STEP):
            rows = pl.ds(STEP * turn, STEP)
            total = sums_of({q: f_v[q, side + 1, rows] for q in range(19)})
            first, frac = level_codes(*total, solid_v[side, rows])
            first_v[pl.ds(NY * side + STEP * turn, STEP)] = first
            frac_v[pl.ds(NY * side + STEP * turn, STEP)] = frac
    table_v[...] = jnp.zeros_like(table_v)
    add_regions(first_v, frac_v, region_v, table_v, 64)
    out.start(table_v, table)
    out.finish()


def edge_regions(solid, region, table, part, r1, r2, held, chunks, field, solid_v, region_v, part_v, r_v, first_v, frac_v, table_v, sems_in, sems_out):
    del held
    odd = odd_slab()
    into, out = Copies(sems_in), Copies(sems_out)
    into.start(r1, r_v.at[0])
    into.start(r2, r_v.at[1])
    into.start(part, part_v)
    into.start(table, table_v)
    for side, z in ((0, 0), (1, CZ - 1)):
        into.start(solid.at[0, z], solid_v.at[side])
        into.start(region.at[0, z], region_v.at[pl.ds(NY * side, NY)])
    into.finish()
    for side, z in ((0, 0), (1, CZ - 1)):
        slot = odd if side == 0 else 1 - odd
        home = UP if side == 0 else DOWN
        for j, q in enumerate(home):
            out.start(r_v.at[slot, j], field.at[0, q, z])
        for turn in range(NY // STEP):
            rows = pl.ds(STEP * turn, STEP)
            more = sums_of({q: r_v[slot, j, rows] for j, q in enumerate(home)})
            total = [part_v[side, k, rows] + more[k] for k in range(4)]
            first, frac = level_codes(*total, solid_v[side, rows])
            first_v[pl.ds(NY * side + STEP * turn, STEP)] = first
            frac_v[pl.ds(NY * side + STEP * turn, STEP)] = frac
    add_regions(first_v, frac_v, region_v, table_v, 64)
    for chunk in range(8):
        low, half = LEVELS * (chunk // 2), NX * (chunk % 2)
        out.start(table_v.at[pl.ds(low, LEVELS), pl.ds(half, NX)], chunks.at[chunk])
    out.finish()


def add_samples(chunks, cdf):
    cdf[0] = (jnp.sum(chunks[...], axis=0) * (1.0 / 256.0)).T


HBM = pl.BlockSpec(memory_space=pltpu.HBM)


def call(kernel, name, outs, scratch, copies, flops, data, aliases=None):
    return pl.pallas_call(
        kernel,
        out_shape=[jax.ShapeDtypeStruct(shape, F32) for shape in outs],
        in_specs=[HBM] * data,
        out_specs=[HBM] * len(outs),
        scratch_shapes=[pltpu.VMEM(shape, kind) for shape, kind in scratch]
        + [pltpu.SemaphoreType.DMA((copies[0],)), pltpu.SemaphoreType.DMA((copies[1],))],
        input_output_aliases=aliases or {},
        compiler_params=pltpu.CompilerParams(vmem_limit_bytes=VMEM_BYTES),
        cost_estimate=pl.CostEstimate(flops=flops, bytes_accessed=4000000, transcendentals=0),
        name=name,
    )


def per_device(deviation, solid, region):
    i32 = jnp.int32
    slabs = lax.axis_size("slab")
    plane = (NY, NX)
    five, nine = (5,) + plane, (9,) + plane
    whole = (1, 19, CZ) + plane
    far = [(i, (i + 1) % slabs if i % 2 else (i - 1) % slabs) for i in range(slabs)]
    near = [(i, i ^ 1) for i in range(slabs)]

    def exchange(first, second):
        return lax.ppermute(first, "slab", far), lax.ppermute(second, "slab", near)

    s1, s2, flat, inner = call(
        first_edges,
        "first_edges",
        [five, five, (2,) + nine, (2,) + five],
        [
            ((2, 19) + plane, BF16),
            ((2,) + plane, i32),
            ((2,) + five, F32),
            ((2,) + nine, F32),
            ((2,) + five, F32),
        ],
        (4, 6),
        10000000,
        2,
    )(deviation, solid)
    r1, r2 = exchange(s1, s2)
    edge, field = call(
        first_inside,
        "first_inside",
        [(2,) + five, whole],
        [
            ((19, 2) + plane, BF16),
            ((2,) + plane, i32),
            ((2, 19) + plane, F32),
            ((2,) + five, F32),
            ((19, CZ) + plane, F32),
        ],
        (12, 13),
        20000000,
        3,
    )(deviation, solid, inner)
    s1, s2, field = call(
        second_edges,
        "second_edges",
        [five, five, whole],
        [
            ((2,) + plane, i32),
            ((2,) + nine, F32),
            ((2,) + five, F32),
            ((2,) + five, F32),
            ((2,) + five, F32),
            ((19, 2) + plane, F32),
        ],
        (6, 16),
        10000000,
        6,
        {5: 2},
    )(solid, flat, edge, r1, r2, field)
    r1, r2 = exchange(s1, s2)
    rows = (2 * NY, NX)
    table, part = call(
        inside_regions,
        "inside_regions",
        [(256, 256), (2, 4) + plane],
        [
            ((19, CZ) + plane, F32),
            ((2,) + plane, i32),
            (rows, i32),
            (rows, F32),
            (rows, F32),
            ((256, 256), F32),
            ((2, 4) + plane, F32),
        ],
        (22, 2),
        2000000000,
        3,
    )(field, solid, region)
    chunks, field = call(
        edge_regions,
        "edge_regions",
        [(8, LEVELS, NX), whole],
        [
            ((2,) + plane, i32),
            (rows, i32),
            ((2, 4) + plane, F32),
            ((2,) + five, F32),
            (rows, F32),
            (rows, F32),
            ((256, 256), F32),
        ],
        (8, 18),
        2000000000,
        7,
        {6: 1},
    )(solid, region, table, part, r1, r2, field)
    chunks = lax.all_to_all(chunks, "sample", 0, 0)
    cdf = pl.pallas_call(
        add_samples,
        out_shape=jax.ShapeDtypeStruct((1, NX, LEVELS), F32),
        name="add_samples",
    )(chunks)
    return field, cdf


def solution(mesh):
    return jax.shard_map(
        per_device,
        mesh=mesh,
        in_specs=(
            P("sample", None, "slab", None, None),
            P("sample", "slab", None, None),
            P("sample", "slab", None, None),
        ),
        out_specs=(P("sample", None, "slab", None, None), P("slab", "sample", None)),
        check_vma=False,
    )
```

profile of v0, /device:TPU:1, one launch (start us, length us, event | category | flops | bytes accessed | tf_op | source)
XLA Modules:
  0.0 72.7 jit_solution(5532729500700147235)
XLA Ops:
  0.6 0.0 copy-start
  0.6 1.3 %copy-done = bf16[1,19,4,64,128]{4,3,2,1,0:T(8,128)(2,1)S(1)} copy-done((bf16[1,19,4,64,128]{4,3,2,1,0:T(8,128)(2,1)S(1)}, bf16[1,19,4,64,128]{4,3,2,1,0:T(8,128)(2,1)}, u32[]{:S(2)}) %copy-start) | copy-done | bytes 1245208
  1.9 0.9 %copy-done.2 = s32[1,4,64,128]{3,2,1,0:T(8,128)S(1)} copy-done((s32[1,4,64,128]{3,2,1,0:T(8,128)S(1)}, s32[1,4,64,128]{3,2,1,0:T(8,128)}, u32[]{:S(2)}) %copy-start.2) | copy-done | bytes 131096
  2.8 1.9 %first_edges.1 = (f32[5,64,128]{2,1,0:T(8,128)S(1)}, f32[5,64,128]{2,1,0:T(8,128)S(1)}, f32[2,9,64,128]{3,2,1,0:T(8,128)S(1)}, f32[2,5,64,128]{3,2,1,0:T(8,128)S(1)}) custom-call(bf16[1,19,4,64,128]{4,3,2,1,0:T(8,128)(2,1)S(1)} %copy-done, s32[1,4,64,128]{3,2,1,0:T(8,128)S(1)} %copy-done.2), custom_call_target="tpu_custom_call" | custom-call | flops 10000000 | bytes 4000000 | tf_op jit(solution)/shard_map/first_edges/pallas_call | solution.py:440
  4.7 16.6 %collective-permute-start = (f32[5,64,128]{2,1,0:T(8,128)S(1)}, f32[5,64,128]{2,1,0:T(8,128)S(1)}, u32[]{:S(2)}, u32[]{:S(2)}) collective-permute-start(f32[5,64,128]{2,1,0:T(8,128)S(1)} %get-tuple-element.18), channel_id=1, source_target_pairs={{0,63},{1,2},{2,1},{3,4},{4,3},{5,6},{6,5},{7,8},{8,7},{9,10},{10,... | collective-permute-start | bytes 491528 | tf_op jit(solution)/shard_map/ppermute | solution.py:438
  21.3 1.9 %collective-permute-start.1 = (f32[5,64,128]{2,1,0:T(8,128)S(1)}, f32[5,64,128]{2,1,0:T(8,128)S(1)}, u32[]{:S(2)}, u32[]{:S(2)}) collective-permute-start(f32[5,64,128]{2,1,0:T(8,128)S(1)} %get-tuple-element.19), channel_id=1, source_target_pairs={{0,1},{1,0},{2,3},{3,2},{4,5},{5,4},{6,7},{7,6},{8,9},{9,8},{10,11... | collective-permute-start | bytes 491528 | tf_op jit(solution)/shard_map/ppermute | solution.py:438
  23.2 0.0 copy-start.4
  23.3 3.1 %first_inside.1 = (f32[2,5,64,128]{3,2,1,0:T(8,128)S(1)}, f32[1,19,4,64,128]{4,3,2,1,0:T(8,128)}) custom-call(bf16[1,19,4,64,128]{4,3,2,1,0:T(8,128)(2,1)S(1)} %copy-done, s32[1,4,64,128]{3,2,1,0:T(8,128)S(1)} %copy-done.2, f32[2,5,64,128]{3,2,1,0:T(8,128)S(1)} %get-tuple-element.16.inner), custom_call_target="tpu_custom_call" | custom-call | flops 20000000 | bytes 4000000 | tf_op jit(solution)/shard_map/first_inside/pallas_call | solution.py:456
  26.4 0.0 collective-permute-done.r1
  26.4 1.5 %collective-permute-done.1.r2 = f32[5,64,128]{2,1,0:T(8,128)S(1)} collective-permute-done((f32[5,64,128]{2,1,0:T(8,128)S(1)}, f32[5,64,128]{2,1,0:T(8,128)S(1)}, u32[]{:S(2)}, u32[]{:S(2)}) %collective-permute-start.1) | collective-permute-done | bytes 163872 | tf_op jit(solution)/shard_map/ppermute | solution.py:438
  28.0 0.0 copy-done.3
  28.0 2.2 %second_edges.1 = (f32[5,64,128]{2,1,0:T(8,128)S(1)}, f32[5,64,128]{2,1,0:T(8,128)S(1)}, f32[1,19,4,64,128]{4,3,2,1,0:T(8,128)}) custom-call(s32[1,4,64,128]{3,2,1,0:T(8,128)S(1)} %copy-done.3, f32[2,9,64,128]{3,2,1,0:T(8,128)S(1)} %get-tuple-element.15.flat, f32[2,5,64,128]{3,2,1,0:T(8,128)S(1)} %get-tuple-element.17.edge, ...), custom_call_target="tpu_custom_call", output_to_operand_aliasing={{2}: (5, {})} | custom-call | flops 10000000 | bytes 4000000 | tf_op jit(solution)/shard_map/second_edges/pallas_call | solution.py:471
  30.2 11.2 %collective-permute-start.2 = (f32[5,64,128]{2,1,0:T(8,128)S(1)}, f32[5,64,128]{2,1,0:T(8,128)S(1)}, u32[]{:S(2)}, u32[]{:S(2)}) collective-permute-start(f32[5,64,128]{2,1,0:T(8,128)S(1)} %get-tuple-element.24), channel_id=1, source_target_pairs={{0,63},{1,2},{2,1},{3,4},{4,3},{5,6},{6,5},{7,8},{8,7},{9,10},{10,... | collective-permute-start | bytes 491528 | tf_op jit(solution)/shard_map/ppermute | solution.py:438
  41.4 1.9 %collective-permute-start.3 = (f32[5,64,128]{2,1,0:T(8,128)S(1)}, f32[5,64,128]{2,1,0:T(8,128)S(1)}, u32[]{:S(2)}, u32[]{:S(2)}) collective-permute-start(f32[5,64,128]{2,1,0:T(8,128)S(1)} %get-tuple-element.25), channel_id=1, source_target_pairs={{0,1},{1,0},{2,3},{3,2},{4,5},{5,4},{6,7},{7,6},{8,9},{9,8},{10,11... | collective-permute-start | bytes 491528 | tf_op jit(solution)/shard_map/ppermute | solution.py:438
  43.3 0.0 copy-done.4
  43.4 0.0 copy-start.1
  43.4 1.7 %copy-done.1 = f32[1,19,4,64,128]{4,3,2,1,0:T(8,128)S(1)} copy-done((f32[1,19,4,64,128]{4,3,2,1,0:T(8,128)S(1)}, f32[1,19,4,64,128]{4,3,2,1,0:T(8,128)}, u32[]{:S(2)}) %copy-start.1) | copy-done | bytes 2490392
  45.1 6.5 %inside_regions.1 = (f32[256,256]{1,0:T(8,128)S(1)}, f32[2,4,64,128]{3,2,1,0:T(8,128)S(1)}) custom-call(f32[1,19,4,64,128]{4,3,2,1,0:T(8,128)S(1)} %copy-done.1, s32[1,4,64,128]{3,2,1,0:T(8,128)S(1)} %copy-done.3, s32[1,4,64,128]{3,2,1,0:T(8,128)S(1)} %copy-done.4), custom_call_target="tpu_custom_call" | custom-call | flops 2000000000 | bytes 4000000 | tf_op jit(solution)/shard_map/inside_regions/pallas_call | solution.py:490
  51.5 0.0 collective-permute-done.2.r1
  51.5 0.0 collective-permute-done.3.r2
  51.5 3.6 %edge_regions.1 = (f32[8,64,128]{2,1,0:T(8,128)S(1)}, f32[1,19,4,64,128]{4,3,2,1,0:T(8,128)}) custom-call(s32[1,4,64,128]{3,2,1,0:T(8,128)S(1)} %copy-done.3, s32[1,4,64,128]{3,2,1,0:T(8,128)S(1)} %copy-done.4, f32[256,256]{1,0:T(8,128)S(1)} %get-tuple-element.22.table, ...), custom_call_target="tpu_custom_call", output_to_operand_aliasing={{1}: (6, {})} | custom-call | flops 2000000000 | bytes 4000000 | tf_op jit(solution)/shard_map/edge_regions/pallas_call | solution.py:507
  55.2 14.4 %all_to_all.5.chunks = f32[8,64,128]{2,1,0:T(8,128)} all-to-all(f32[8,64,128]{2,1,0:T(8,128)S(1)} %get-tuple-element.27), channel_id=1, replica_groups=mesh['sample'=8,'slab'=64] {'sample'}, dimensions={0} | all-to-all | bytes 524288 | tf_op jit(solution)/shard_map/all_to_all | solution.py:525
  69.5 1.7 %add_samples.1 = f32[1,128,64]{2,1,0:T(8,128)} custom-call(f32[8,64,128]{2,1,0:T(8,128)} %all_to_all.5.chunks), custom_call_target="tpu_custom_call" | custom-call | tf_op jit(solution)/shard_map/add_samples/pallas_call | solution.py:526
  71.2 1.5 %copy.7 = f32[1,128,64]{1,2,0:T(8,128)} copy(f32[1,128,64]{2,1,0:T(8,128)} %add_samples.1) | data formatting | bytes 65536
  (2 shorter events, 0.0 us)
Async XLA Ops:
  0.6 1.3 %copy-start = (bf16[1,19,4,64,128]{4,3,2,1,0:T(8,128)(2,1)S(1)}, bf16[1,19,4,64,128]{4,3,2,1,0:T(8,128)(2,1)}, u32[]{:S(2)}) copy-start(bf16[1,19,4,64,128]{4,3,2,1,0:T(8,128)(2,1)} %dev.3) | copy-start | bytes 3735556
  1.9 0.9 %copy-start.2 = (s32[1,4,64,128]{3,2,1,0:T(8,128)S(1)}, s32[1,4,64,128]{3,2,1,0:T(8,128)}, u32[]{:S(2)}) copy-start(s32[1,4,64,128]{3,2,1,0:T(8,128)} %solid.9) | copy-start | bytes 393220
  2.8 25.1 %copy-start.3 = (s32[1,4,64,128]{3,2,1,0:T(8,128)S(1)}, s32[1,4,64,128]{3,2,1,0:T(8,128)}, u32[]{:S(2)}) copy-start(s32[1,4,64,128]{3,2,1,0:T(8,128)} %solid.9) | copy-start | bytes 393220
  4.7 21.7 %collective-permute-start = (f32[5,64,128]{2,1,0:T(8,128)S(1)}, f32[5,64,128]{2,1,0:T(8,128)S(1)}, u32[]{:S(2)}, u32[]{:S(2)}) collective-permute-start(f32[5,64,128]{2,1,0:T(8,128)S(1)} %get-tuple-element.18), channel_id=1, source_target_pairs={{0,63},{1,2},{2,1},{3,4},{4,3},{5,6},{6,5},{7,8},{8,7},{9,10},{10,... | collective-permute-start | bytes 491528 | tf_op jit(solution)/shard_map/ppermute | solution.py:438
  21.3 6.6 %collective-permute-start.1 = (f32[5,64,128]{2,1,0:T(8,128)S(1)}, f32[5,64,128]{2,1,0:T(8,128)S(1)}, u32[]{:S(2)}, u32[]{:S(2)}) collective-permute-start(f32[5,64,128]{2,1,0:T(8,128)S(1)} %get-tuple-element.19), channel_id=1, source_target_pairs={{0,1},{1,0},{2,3},{3,2},{4,5},{5,4},{6,7},{7,6},{8,9},{9,8},{10,11... | collective-permute-start | bytes 491528 | tf_op jit(solution)/shard_map/ppermute | solution.py:438
  23.2 20.1 %copy-start.4 = (s32[1,4,64,128]{3,2,1,0:T(8,128)S(1)}, s32[1,4,64,128]{3,2,1,0:T(8,128)}, u32[]{:S(2)}) copy-start(s32[1,4,64,128]{3,2,1,0:T(8,128)} %region.3) | copy-start | bytes 393220
  30.2 21.3 %collective-permute-start.2 = (f32[5,64,128]{2,1,0:T(8,128)S(1)}, f32[5,64,128]{2,1,0:T(8,128)S(1)}, u32[]{:S(2)}, u32[]{:S(2)}) collective-permute-start(f32[5,64,128]{2,1,0:T(8,128)S(1)} %get-tuple-element.24), channel_id=1, source_target_pairs={{0,63},{1,2},{2,1},{3,4},{4,3},{5,6},{6,5},{7,8},{8,7},{9,10},{10,... | collective-permute-start | bytes 491528 | tf_op jit(solution)/shard_map/ppermute | solution.py:438
  41.4 10.1 %collective-permute-start.3 = (f32[5,64,128]{2,1,0:T(8,128)S(1)}, f32[5,64,128]{2,1,0:T(8,128)S(1)}, u32[]{:S(2)}, u32[]{:S(2)}) collective-permute-start(f32[5,64,128]{2,1,0:T(8,128)S(1)} %get-tuple-element.25), channel_id=1, source_target_pairs={{0,1},{1,0},{2,3},{3,2},{4,5},{5,4},{6,7},{7,6},{8,9},{9,8},{10,11... | collective-permute-start | bytes 491528 | tf_op jit(solution)/shard_map/ppermute | solution.py:438
  43.4 1.7 %copy-start.1 = (f32[1,19,4,64,128]{4,3,2,1,0:T(8,128)S(1)}, f32[1,19,4,64,128]{4,3,2,1,0:T(8,128)}, u32[]{:S(2)}) copy-start(f32[1,19,4,64,128]{4,3,2,1,0:T(8,128)} %get-tuple-element.21.field.held) | copy-start | bytes 7471108
where the time goes:
time: 73.2 us; the launch traced here: 72.7 us
  starting transfers between devices  31.6 us (43%)
  Pallas kernels  19 us (26%)
  blocking collectives  14.4 us (20%)
  local copies, waits for them, and re-layouts  5.43 us (7%)
  waiting for transfers between devices  1.55 us (2%)
  between operations  0.76 us (1%)
    ppermute x2, starting transfers between devices, exchange(): lax.ppermute(first, 'slab', far)  27.8 us
    all_to_all x1, blocking collectives, per_device(): chunks = lax.all_to_all(chunks, 'sample', 0, 0)  14.4 us
    pallas_call x1, Pallas kernels, per_device(): call(inside_regions, 'inside_regions', [(256, 256), (2, 4) + plane], [((1...  6.45 us
    unnamed x11, local copies, waits for them, and re-layouts  5.43 us
    ppermute x2, starting transfers between devices, exchange(): lax.ppermute(second, 'slab', near)  3.84 us
    pallas_call x1, Pallas kernels, per_device(): call(edge_regions, 'edge_regions', [(8, LEVELS, NX), whole], [((2,) + pla...  3.63 us
    pallas_call x1, Pallas kernels, per_device(): call(first_inside, 'first_inside', [(2,) + five, whole], [((19, 2) + plan...  3.15 us
    pallas_call x1, Pallas kernels, per_device(): call(second_edges, 'second_edges', [five, five, whole], [((2,) + plane, i...  2.23 us
  transfers between devices with their start and end apart: 4, of which 1 were waited for; matrix products, arithmetic and copies ran while one was open for 0% of the time, Pallas kernels for 13%

commit v1 on v0

v1 whole, which is shorter than its diff:
```python
import jax
import jax.numpy as jnp
from jax import lax
from jax.experimental import pallas as pl
from jax.experimental.pallas import tpu as pltpu
from jax.sharding import PartitionSpec as P

LEVELS = 64
AMPLITUDE = 0.3
SPEED_TOP = 0.12
MOVES = [
    (0, 0, 0),
    (1, 0, 0),
    (-1, 0, 0),
    (0, 1, 0),
    (0, -1, 0),
    (0, 0, 1),
    (0, 0, -1),
    (1, 1, 0),
    (-1, -1, 0),
    (1, -1, 0),
    (-1, 1, 0),
    (1, 0, 1),
    (-1, 0, -1),
    (1, 0, -1),
    (-1, 0, 1),
    (0, 1, 1),
    (0, -1, -1),
    (0, 1, -1),
    (0, -1, 1),
]
OPPOSITE = [0, 2, 1, 4, 3, 6, 5, 8, 7, 10, 9, 12, 11, 14, 13, 16, 15, 18, 17]
WEIGHTS = [1.0 / 3.0] + [1.0 / 18.0] * 6 + [1.0 / 36.0] * 12
FLAT = [q for q in range(19) if MOVES[q][2] == 0]
UP = [q for q in range(19) if MOVES[q][2] == 1]
DOWN = [q for q in range(19) if MOVES[q][2] == -1]
FLAT_RUNS = ((0, 5), (7, 4))
EDGES = ((0, 0), (1, 3))
AWAY, HOME = (DOWN, UP), (UP, DOWN)
NX, NY, CZ = 128, 64, 4
STEP = 8
VMEM_BYTES = 40 * 1024 * 1024
BF16 = jnp.bfloat16
F32 = jnp.float32


def collide(f, rock):
    sx, sy, sz = f[1] + f[2], f[3] + f[4], f[5] + f[6]
    s7, s9, s11 = f[7] + f[8], f[9] + f[10], f[11] + f[12]
    s13, s15, s17 = f[13] + f[14], f[15] + f[16], f[17] + f[18]
    dx, dy, dz = f[1] - f[2], f[3] - f[4], f[5] - f[6]
    d7, d9, d11 = f[7] - f[8], f[9] - f[10], f[11] - f[12]
    d13, d15, d17 = f[13] - f[14], f[15] - f[16], f[17] - f[18]
    sxy, sxz, syz = s7 + s9, s11 + s13, s15 + s17
    one, two = sx + (sy + sz), sxy + (sxz + syz)
    rho = f[0] + one + two
    ax, bx = d7 + d9, d11 + d13
    ay, by = d15 + d17, d7 - d9
    az, bz = d11 - d13, d15 - d17
    jx, jy, jz = dx + (ax + bx), dy + (ay + by), dz + (az + bz)
    inv = 1.0 / rho
    ux, uy, uz = jx * inv, jy * inv, jz * inv
    xx, yy, zz = jx * ux, jy * uy, jz * uz
    square = xx + yy + zz
    e = (1.19 * 19 / 2394) * (two - f[0] - square)
    eps = (1.4 / 252) * (9.0 * f[0] - 7.0 * one - 2.0 * two + 5.5 * square)
    even0 = 12.0 * eps - 30.0 * e
    base1 = -11.0 * e - 4.0 * eps
    base2 = 8.0 * e + eps
    p1, p2, px = 3.0 * sx - one, two - 3.0 * syz, 3.0 * xx - square
    pxx = (1.25 / 36) * (p1 + p2 - px)
    pixx = (1.4 / 72) * (p2 - 2.0 * p1 + 0.5 * px)
    w1, w2, pw = sy - sz, sxy - sxz, yy - zz
    pww = (1.25 / 12) * (w1 + w2 - pw)
    piww = (1.4 / 24) * (w2 - 2.0 * w1 + 0.5 * pw)
    pxy = (1.25 / 4) * (s7 - s9 - jx * uy)
    pxz = (1.25 / 4) * (s11 - s13 - jx * uz)
    pyz = (1.25 / 4) * (s15 - s17 - jy * uz)
    ua, va = pxx - 2.0 * pixx, pxx + pixx
    ub, vb = pww - 2.0 * piww, pww + piww
    qx = 0.05 * jx - 0.15 * dx
    qy = 0.05 * jy - 0.15 * dy
    qz = 0.05 * jz - 0.15 * dz
    mx = (1.98 / 8) * (ax - bx)
    my = (1.98 / 8) * (ay - by)
    mz = (1.98 / 8) * (az - bz)
    xp, xm, yp, ym = qx + mx, qx - mx, qy + my, qy - my
    zp, zm = qz + mz, qz - mz
    rest = base1 - ua
    xy, xz, yz = base2 + va + vb, base2 + va - vb, base2 - 2.0 * va
    pairs = {
        1: (base1 + 2.0 * ua, -4.0 * qx),
        3: (rest + ub, -4.0 * qy),
        5: (rest - ub, -4.0 * qz),
        7: (xy + pxy, xp + ym),
        9: (xy - pxy, xp - ym),
        11: (xz + pxz, xm + zp),
        13: (xz - pxz, xm - zp),
        15: (yz + pyz, yp + zm),
        17: (yz - pyz, yp - zm),
    }
    post = [jnp.where(rock, f[0], f[0] - even0)] + [None] * 18
    for q, (even, odd) in pairs.items():
        post[q] = jnp.where(rock, f[q + 1], f[q] - (even + odd))
        post[q + 1] = jnp.where(rock, f[q], f[q + 1] - (even - odd))
    return post


def put(ref, where, turn, value, q):
    cx, cy, _ = MOVES[q]
    if cx:
        value = pltpu.roll(value, cx % NX, 1)
    row = STEP * turn
    last = NY // STEP - 1
    if cy == 0:
        ref[where + (pl.ds(row, STEP),)] = value
    elif cy == 1 and turn == last:
        ref[where + (pl.ds(row + 1, STEP - 1),)] = value[: STEP - 1]
        ref[where + (pl.ds(0, 1),)] = value[STEP - 1 :]
    elif cy == -1 and turn == 0:
        ref[where + (pl.ds(0, STEP - 1),)] = value[1:]
        ref[where + (pl.ds(NY - 1, 1),)] = value[:1]
    else:
        ref[where + (pl.ds(row + cy, STEP),)] = value


def collide_plane(load, solid, dest):
    for turn in range(NY // STEP):
        f = [load(q, turn) for q in range(19)]
        post = collide(f, solid(turn) == 1)
        for q in range(19):
            if dest[q] is not None:
                ref, where = dest[q]
                put(ref, where, turn, post[q], q)


def initial(ref, where):
    def load(q, turn):
        low = turn // 2 * 16
        rows = ref[where(q) + (pl.ds(low, 16),)].astype(F32)
        rows = rows[(turn % 2) * 8 : (turn % 2) * 8 + 8]
        return WEIGHTS[q] + (WEIGHTS[q] * AMPLITUDE) * rows

    return load


def rows_of(ref, where):
    return lambda turn: ref[where + (pl.ds(STEP * turn, STEP),)]


def rows_from(source):
    def load(q, turn):
        ref, where = source[q]
        where = where + (pl.ds(STEP * turn, STEP),)
        if isinstance(ref, tuple):
            return jnp.where(ref[2] == 0, ref[0][where], ref[1][where])
        return ref[where]

    return load


class Copies:
    def __init__(self, sems):
        self.sems = sems
        self.used = 0
        self.open = []

    def start(self, source, target):
        copy = pltpu.make_async_copy(source, target, self.sems.at[self.used])
        self.used += 1
        copy.start()
        self.open.append(copy)
        return copy

    def finish(self):
        for copy in self.open:
            copy.wait()


def odd_slab():
    return lax.rem(lax.axis_index("slab"), 2)


def first_edges(dev, solid, rock, s1, s2, flat, inner, dev_v, s_v, sems):
    odd = odd_slab()
    into = Copies(sems)
    into.start(solid.at[0], rock)
    for side, z in EDGES:
        into.start(dev.at[0, :, z], dev_v.at[side])
    into.open[0].wait()
    for side, z in EDGES:
        into.open[side + 1].wait()
        slot = odd if side == 0 else 1 - odd
        dest = [None] * 19
        for j, q in enumerate(FLAT):
            dest[q] = (flat, (side, j))
        for j, q in enumerate(AWAY[side]):
            dest[q] = (s_v, (slot, j))
        for j, q in enumerate(HOME[side]):
            dest[q] = (inner, (side, j))
        collide_plane(initial(dev_v, lambda q, side=side: (side, q)), rows_of(rock, (z,)), dest)
    s1[...] = s_v[0]
    s2[...] = s_v[1]


def first_inside(dev, solid, inner, edge, sums, field, dev_v, f_v, g_v, sems_in, sems_out):
    into, out = Copies(sems_in), Copies(sems_out)
    into.start(dev.at[0, :, pl.ds(1, 2)], dev_v)
    into.finish()
    for side in range(2):
        dest = [None] * 19
        for q in FLAT:
            dest[q] = (f_v, (side, q))
        for j, q in enumerate(AWAY[side]):
            dest[q] = (edge, (side, j))
        for q in HOME[side]:
            dest[q] = (f_v, (1 - side, q))
        collide_plane(initial(dev_v, lambda q, side=side: (q, side)), rows_of(solid, (side + 1,)), dest)
    for side in range(2):
        source = {q: (f_v, (side, q)) for q in range(19)}
        for j, q in enumerate(HOME[side]):
            source[q] = (inner, (side, j))
        dest = [(g_v, (q, side + 1 + MOVES[q][2])) for q in range(19)]
        collide_plane(rows_from(source), rows_of(solid, (side + 1,)), dest)
    for low, count in FLAT_RUNS:
        run = pl.ds(low, count)
        out.start(g_v.at[run, pl.ds(1, 2)], field.at[0, run, pl.ds(1, 2)])
    for q in DOWN:
        out.start(g_v.at[q, pl.ds(0, 2)], field.at[0, q, pl.ds(0, 2)])
    for q in UP:
        out.start(g_v.at[q, pl.ds(2, 2)], field.at[0, q, pl.ds(2, 2)])
    for z, have in enumerate((DOWN, FLAT + DOWN, FLAT + UP, UP)):
        for turn in range(NY // STEP):
            rows = pl.ds(STEP * turn, STEP)
            for k, value in enumerate(sums_of({q: g_v[q, z, rows] for q in have})):
                sums[z, k, rows] = value
    out.finish()


def second_edges(solid, flat, edge, r1, r2, s1, s2, flat2, inner2, s_v):
    odd = odd_slab()
    for side, z in EDGES:
        slot = odd if side == 0 else 1 - odd
        source, dest = {}, [None] * 19
        for j, q in enumerate(FLAT):
            source[q] = (flat, (side, j))
            dest[q] = (flat2, (side, j))
        for j, q in enumerate(AWAY[side]):
            source[q] = (edge, (side, j))
            dest[q] = (s_v, (slot, j))
        for j, q in enumerate(HOME[side]):
            source[q] = ((r1, r2, slot), (j,))
            dest[q] = (inner2, (side, j))
        collide_plane(rows_from(source), rows_of(solid, (z,)), dest)
    s1[...] = s_v[0]
    s2[...] = s_v[1]


def sums_of(values):
    total = [None] * 4
    for q, value in values.items():
        for axis, sign in enumerate((1,) + MOVES[q]):
            if sign:
                term = value if total[axis] is None else total[axis]
                if total[axis] is None:
                    total[axis] = value if sign > 0 else -value
                else:
                    total[axis] = term + value if sign > 0 else term - value
    return total


def level_codes(rho, jx, jy, jz, solid):
    inv = 1.0 / rho
    ux, uy, uz = jx * inv, jy * inv, jz * inv
    speed = jnp.sqrt(ux * ux + uy * uy + uz * uz)
    place = jnp.clip(speed * (LEVELS / SPEED_TOP) - 1.5, -2.0, 100.0)
    first = jnp.ceil(place)
    return jnp.where(solid == 1, 300.0, first), first - place


def add_regions(first, part, region, planes, total, rows):
    low_plane, step = planes[0], planes[1] - planes[0]

    def body(turn, carry):
        left, right = [], []
        for j in range(rows):
            row = turn * rows + j

            def spread(row):
                return jnp.broadcast_to(row, (16, NX))

            a = spread(first[pl.ds(row, 1), :]).astype(BF16)
            b = spread(part[pl.ds(row, 1), :]).astype(BF16)
            label = spread(region[0, low_plane + step * turn, pl.ds(j, 1), :])
            high = (label >> 8).astype(F32).astype(BF16)
            low = (label & 255).astype(F32).astype(BF16)
            count = lax.broadcasted_iota(jnp.int32, (16, NX), 0).astype(F32).astype(BF16)
            zero, one = jnp.zeros((16, NX), BF16), jnp.ones((16, NX), BF16)
            ramps = [
                jnp.clip((count + BF16(16 * g) - a) + b, BF16(0), BF16(1)) for g in range(LEVELS // 16)
            ]
            left.append(
                jnp.concatenate([jnp.where(high == BF16(h), r, zero) for h in range(4) for r in ramps], 0)
            )
            right.append(
                jnp.concatenate([jnp.where(low == count + BF16(16 * g), one, zero) for g in range(16)], 0)
            )
        total[...] += lax.dot_general(
            jnp.concatenate(left, 1),
            jnp.concatenate(right, 1),
            (((1,), (1,)), ((), ())),
            preferred_element_type=F32,
        )
        return carry

    lax.fori_loop(0, first.shape[0] // rows, body, 0)


def inside_regions(solid, region, sums, flat2, inner2, held, table, part, field, first_v, frac_v, sems):
    del held
    out = Copies(sems)
    for side, z in EDGES:
        for j, (low, count) in ((0, FLAT_RUNS[0]), (FLAT_RUNS[0][1], FLAT_RUNS[1])):
            out.start(flat2.at[side, pl.ds(j, count)], field.at[0, pl.ds(low, count), z])
        for j, q in enumerate(HOME[side]):
            out.start(inner2.at[side, j], field.at[0, q, z + MOVES[q][2]])
    for side, z in EDGES:
        for turn in range(NY // STEP):
            rows = pl.ds(STEP * turn, STEP)
            more = sums_of({q: flat2[side, j, rows] for j, q in enumerate(FLAT)})
            for k in range(4):
                here = sums[z, k, rows]
                part[side, k, rows] = here if more[k] is None else here + more[k]
            more = sums_of({q: inner2[side, j, rows] for j, q in enumerate(HOME[side])})
            total = [sums[side + 1, k, rows] + more[k] for k in range(4)]
            first, frac = level_codes(*total, solid[side + 1, rows])
            first_v[pl.ds(NY * side + STEP * turn, STEP)] = first
            frac_v[pl.ds(NY * side + STEP * turn, STEP)] = frac
    table[...] = jnp.zeros_like(table)
    add_regions(first_v, frac_v, region, (1, 2), table, 64)
    out.finish()


def edge_regions(solid, region, table, part, r1, r2, held, chunks, field, first_v, frac_v, table_v, sems):
    del held
    odd = odd_slab()
    out = Copies(sems)
    for which, ref in ((0, r1), (1, r2)):

        @pl.when(odd == which)
        def _(ref=ref, sem=2 * which):
            for j, q in enumerate(UP):
                pltpu.make_async_copy(ref.at[j], field.at[0, q, 0], sems.at[j]).start()

        @pl.when(odd != which)
        def _(ref=ref):
            for j, q in enumerate(DOWN):
                pltpu.make_async_copy(ref.at[j], field.at[0, q, CZ - 1], sems.at[5 + j]).start()

    for side, z in EDGES:
        slot = odd if side == 0 else 1 - odd
        for turn in range(NY // STEP):
            rows = pl.ds(STEP * turn, STEP)
            load = rows_from({q: ((r1, r2, slot), (j,)) for j, q in enumerate(HOME[side])})
            more = sums_of({q: load(q, turn) for q in HOME[side]})
            total = [part[side, k, rows] + more[k] for k in range(4)]
            first, frac = level_codes(*total, solid[z, rows])
            first_v[pl.ds(NY * side + STEP * turn, STEP)] = first
            frac_v[pl.ds(NY * side + STEP * turn, STEP)] = frac
    table_v[...] = table[...]
    add_regions(first_v, frac_v, region, (0, CZ - 1), table_v, 64)
    for chunk in range(8):
        low, half = LEVELS * (chunk // 2), NX * (chunk % 2)
        chunks[chunk] = table_v[low : low + LEVELS, half : half + NX]
    for j in range(5):
        pltpu.make_async_copy(r1.at[j], field.at[0, UP[j], 0], sems.at[j]).wait()
        pltpu.make_async_copy(r1.at[j], field.at[0, DOWN[j], CZ - 1], sems.at[5 + j]).wait()


HBM = pl.BlockSpec(memory_space=pltpu.HBM)
VMEM = pl.BlockSpec(memory_space=pltpu.VMEM)


def call(kernel, places, outs, scratch, copies, flops, aliases=None, room=VMEM_BYTES, kinds=None):
    specs = [HBM if place == "H" else VMEM for place in places]
    data = len(places) - len(outs)
    return pl.pallas_call(
        kernel,
        out_shape=[jax.ShapeDtypeStruct(shape, kind) for shape, kind in zip(outs, kinds or [F32] * len(outs))],
        in_specs=specs[:data],
        out_specs=specs[data:],
        scratch_shapes=[pltpu.VMEM(shape, dtype) for shape, dtype in scratch]
        + [pltpu.SemaphoreType.DMA((count,)) for count in copies],
        input_output_aliases=aliases or {},
        compiler_params=pltpu.CompilerParams(vmem_limit_bytes=room),
        cost_estimate=pl.CostEstimate(flops=flops, bytes_accessed=4000000, transcendentals=0),
        name=kernel.__name__,
    )


def per_device(deviation, solid, region):
    i32 = jnp.int32
    slabs = lax.axis_size("slab")
    plane = (NY, NX)
    five, nine = (5,) + plane, (9,) + plane
    whole = (1, 19, CZ) + plane
    rows = (2 * NY, NX)
    far = [(i, (i + 1) % slabs if i % 2 else (i - 1) % slabs) for i in range(slabs)]
    near = [(i, i ^ 1) for i in range(slabs)]

    def exchange(first, second):
        return lax.ppermute(first, "slab", far), lax.ppermute(second, "slab", near)

    deviation = pltpu.with_memory_space_constraint(deviation, pltpu.HBM)
    solid = pltpu.with_memory_space_constraint(solid, pltpu.HBM)
    rock, s1, s2, flat, inner = call(
        first_edges,
        "HHVVVVV",
        [(CZ,) + plane, five, five, (2,) + nine, (2,) + five],
        [((2, 19) + plane, BF16), ((2,) + five, F32)],
        (3,),
        10000000,
        kinds=(i32, F32, F32, F32, F32),
    )(deviation, solid)
    r1, r2 = exchange(s1, s2)
    edge, sums, field = call(
        first_inside,
        "HVVVVH",
        [(2,) + five, (CZ, 4) + plane, whole],
        [((19, 2) + plane, BF16), ((2, 19) + plane, F32), ((19, CZ) + plane, F32)],
        (1, 12),
        20000000,
    )(deviation, rock, inner)
    s1, s2, flat, inner = call(
        second_edges,
        "VVVVVVVVV",
        [five, five, (2,) + nine, (2,) + five],
        [((2,) + five, F32)],
        (),
        10000000,
    )(rock, flat, edge, r1, r2)
    r1, r2 = exchange(s1, s2)
    table, part, field = call(
        inside_regions,
        "VVVVVHVVH",
        [(256, 256), (2, 4) + plane, whole],
        [(rows, F32), (rows, F32)],
        (14,),
        2000000000,
        {5: 2},
    )(rock, region, sums, flat, inner, field)
    chunks, field = call(
        edge_regions,
        "VVVVVVHVH",
        [(8, LEVELS, NX), whole],
        [(rows, F32), (rows, F32), ((256, 256), F32)],
        (10,),
        2000000000,
        {6: 1},
    )(rock, region, table, part, r1, r2, field)
    chunks = lax.all_to_all(chunks, "sample", 0, 0)
    cdf = jnp.sum(chunks, axis=0) * (1.0 / 256.0)
    return field, jnp.swapaxes(cdf, 0, 1)[None]


def solution(mesh):
    return jax.shard_map(
        per_device,
        mesh=mesh,
        in_specs=(
            P("sample", None, "slab", None, None),
            P("sample", "slab", None, None),
            P("sample", "slab", None, None),
        ),
        out_specs=(P("sample", None, "slab", None, None), P("slab", "sample", None)),
        check_vma=False,
    )
```

time: 73.2 us -> 62.5 us (0.85)
  Pallas kernels: 19 us -> 11.6 us
  local copies, waits for them, and re-layouts: 5.43 us -> 0.01 us
  waiting for transfers between devices: 1.55 us -> 2.49 us
    pallas_call x6 -> x5, Pallas kernels: 19 us -> 11.6 us  [the longest x1 3.45 us: per_device(): call(first_inside, 'HVVVVH', [(2,) + five, (CZ, 4) + plane, whole], [((19...]
    unnamed x11 -> x2, local copies, waits for them, and re-layouts: 5.43 us -> 0.01 us
    ppermute x2, waiting for transfers between devices: 1.54 us -> 2.48 us  [exchange(): lax.ppermute(second, 'slab', near)]
  transfers between devices with their start and end apart: 4 -> 4, of which waited for: 1 -> 2; matrix products, arithmetic and copies ran while one was open for 0% -> 0% of each run, Pallas kernels for 13% -> 10%
where the time goes in v1:
time: 62.5 us; the launch traced here: 62.2 us
  starting transfers between devices  31.6 us (51%)
  blocking collectives  15.1 us (24%)
  Pallas kernels  11.6 us (19%)
  waiting for transfers between devices  2.49 us (4%)
  between operations  0.73 us (1%)
  other arithmetic  0.64 us (1%)
    ppermute x2, starting transfers between devices, exchange(): lax.ppermute(first, 'slab', far)  27.8 us
    all_to_all x1, blocking collectives, per_device(): chunks = lax.all_to_all(chunks, 'sample', 0, 0)  15.1 us
    ppermute x2, starting transfers between devices, exchange(): lax.ppermute(second, 'slab', near)  3.84 us
    pallas_call x1, Pallas kernels, per_device(): call(first_inside, 'HVVVVH', [(2,) + five, (CZ, 4) + plane, whole], [((19...  3.45 us
    pallas_call x1, Pallas kernels, per_device(): call(inside_regions, 'VVVVVHVVH', [(256, 256), (2, 4) + plane, whole], [(...  2.87 us
    pallas_call x1, Pallas kernels, per_device(): call(edge_regions, 'VVVVVVHVH', [(8, LEVELS, NX), whole], [(rows, F32), (...  2.8 us
    ppermute x2, waiting for transfers between devices, exchange(): lax.ppermute(second, 'slab', near)  2.48 us
    pallas_call x1, Pallas kernels, per_device(): call(first_edges, 'HHVVVVV', [(CZ,) + plane, five, five, (2,) + nine, (2,...  1.91 us
  transfers between devices with their start and end apart: 4, of which 2 were waited for; matrix products, arithmetic and copies ran while one was open for 0% of the time, Pallas kernels for 10%

profile of v1, /device:TPU:1, one launch (start us, length us, event | category | flops | bytes accessed | tf_op | source)
XLA Modules:
  0.0 62.2 jit_solution(13630542221624197390)
XLA Ops:
  0.6 0.0 copy-start
  0.6 1.9 %first_edges.1 = (s32[4,64,128]{2,1,0:T(8,128)S(1)}, f32[5,64,128]{2,1,0:T(8,128)S(1)}, f32[5,64,128]{2,1,0:T(8,128)S(1)}, f32[2,9,64,128]{3,2,1,0:T(8,128)S(1)}, f32[2,5,64,128]{3,2,1,0:T(8,128)S(1)}) custom-call(bf16[1,19,4,64,128]{4,3,2,1,0:T(8,128)(2,1)} %dev.3, s32[1,4,64,128]{3,2,1,0:T(8,128)} %solid.1), custom_call_target="tpu_custom_call" | custom-call | flops 10000000 | bytes 4000000 | tf_op jit(solution)/shard_map/first_edges/pallas_call | solution.py:416
  2.6 16.6 %collective-permute-start = (f32[5,64,128]{2,1,0:T(8,128)S(1)}, f32[5,64,128]{2,1,0:T(8,128)S(1)}, u32[]{:S(2)}, u32[]{:S(2)}) collective-permute-start(f32[5,64,128]{2,1,0:T(8,128)S(1)} %get-tuple-element.24), channel_id=1, source_target_pairs={{0,63},{1,2},{2,1},{3,4},{4,3},{5,6},{6,5},{7,8},{8,7},{9,10},{10,... | collective-permute-start | bytes 491528 | tf_op jit(solution)/shard_map/ppermute | solution.py:412
  19.1 1.9 %collective-permute-start.1 = (f32[5,64,128]{2,1,0:T(8,128)S(1)}, f32[5,64,128]{2,1,0:T(8,128)S(1)}, u32[]{:S(2)}, u32[]{:S(2)}) collective-permute-start(f32[5,64,128]{2,1,0:T(8,128)S(1)} %get-tuple-element.25), channel_id=1, source_target_pairs={{0,1},{1,0},{2,3},{3,2},{4,5},{5,4},{6,7},{7,6},{8,9},{9,8},{10,11... | collective-permute-start | bytes 491528 | tf_op jit(solution)/shard_map/ppermute | solution.py:412
  21.1 3.5 %first_inside.1 = (f32[2,5,64,128]{3,2,1,0:T(8,128)S(1)}, f32[4,4,64,128]{3,2,1,0:T(8,128)S(1)}, f32[1,19,4,64,128]{4,3,2,1,0:T(8,128)}) custom-call(bf16[1,19,4,64,128]{4,3,2,1,0:T(8,128)(2,1)} %dev.3, s32[4,64,128]{2,1,0:T(8,128)S(1)} %get-tuple-element.19.solid, f32[2,5,64,128]{3,2,1,0:T(8,128)S(1)} %get-tuple-element.20.inner), custom_call_target="tpu_custom_call" | custom-call | flops 20000000 | bytes 4000000 | tf_op jit(solution)/shard_map/first_inside/pallas_call | solution.py:426
  24.5 0.0 collective-permute-done.r1
  24.5 1.2 %collective-permute-done.1.r2 = f32[5,64,128]{2,1,0:T(8,128)S(1)} collective-permute-done((f32[5,64,128]{2,1,0:T(8,128)S(1)}, f32[5,64,128]{2,1,0:T(8,128)S(1)}, u32[]{:S(2)}, u32[]{:S(2)}) %collective-permute-start.1) | collective-permute-done | bytes 163872 | tf_op jit(solution)/shard_map/ppermute | solution.py:412
  25.8 0.6 second_edges.1
  26.4 11.2 %collective-permute-start.2 = (f32[5,64,128]{2,1,0:T(8,128)S(1)}, f32[5,64,128]{2,1,0:T(8,128)S(1)}, u32[]{:S(2)}, u32[]{:S(2)}) collective-permute-start(f32[5,64,128]{2,1,0:T(8,128)S(1)} %get-tuple-element.31), channel_id=1, source_target_pairs={{0,63},{1,2},{2,1},{3,4},{4,3},{5,6},{6,5},{7,8},{8,7},{9,10},{10,... | collective-permute-start | bytes 491528 | tf_op jit(solution)/shard_map/ppermute | solution.py:412
  37.6 1.9 %collective-permute-start.3 = (f32[5,64,128]{2,1,0:T(8,128)S(1)}, f32[5,64,128]{2,1,0:T(8,128)S(1)}, u32[]{:S(2)}, u32[]{:S(2)}) collective-permute-start(f32[5,64,128]{2,1,0:T(8,128)S(1)} %get-tuple-element.32), channel_id=1, source_target_pairs={{0,1},{1,0},{2,3},{3,2},{4,5},{5,4},{6,7},{7,6},{8,9},{9,8},{10,11... | collective-permute-start | bytes 491528 | tf_op jit(solution)/shard_map/ppermute | solution.py:412
  39.5 0.0 copy-done
  39.5 2.9 %inside_regions.1 = (f32[256,256]{1,0:T(8,128)S(1)}, f32[2,4,64,128]{3,2,1,0:T(8,128)S(1)}, f32[1,19,4,64,128]{4,3,2,1,0:T(8,128)}) custom-call(s32[4,64,128]{2,1,0:T(8,128)S(1)} %get-tuple-element.19.solid, s32[1,4,64,128]{3,2,1,0:T(8,128)S(1)} %copy-done, f32[4,4,64,128]{3,2,1,0:T(8,128)S(1)} %get-tuple-element.21.sums, ...), custom_call_target="tpu_custom_call", output_to_operand_aliasing={{2}: (5, {})} | custom-call | flops 2000000000 | bytes 4000000 | tf_op jit(solution)/shard_map/inside_regions/pallas_call | solution.py:443
  42.4 0.0 collective-permute-done.2.r1
  42.4 1.2 %collective-permute-done.3.r2 = f32[5,64,128]{2,1,0:T(8,128)S(1)} collective-permute-done((f32[5,64,128]{2,1,0:T(8,128)S(1)}, f32[5,64,128]{2,1,0:T(8,128)S(1)}, u32[]{:S(2)}, u32[]{:S(2)}) %collective-permute-start.3) | collective-permute-done | bytes 163872 | tf_op jit(solution)/shard_map/ppermute | solution.py:412
  43.6 2.8 %edge_regions.1 = (f32[8,64,128]{2,1,0:T(8,128)S(1)}, f32[1,19,4,64,128]{4,3,2,1,0:T(8,128)}) custom-call(s32[4,64,128]{2,1,0:T(8,128)S(1)} %get-tuple-element.19.solid, s32[1,4,64,128]{3,2,1,0:T(8,128)S(1)} %copy-done, f32[256,256]{1,0:T(8,128)S(1)} %get-tuple-element.29.table, ...), custom_call_target="tpu_custom_call", output_to_operand_aliasing={{1}: (6, {})} | custom-call | flops 2000000000 | bytes 4000000 | tf_op jit(solution)/shard_map/edge_regions/pallas_call | solution.py:452
  46.4 15.1 %all_to_all.5 = f32[8,64,128]{2,1,0:T(8,128)S(1)} all-to-all(f32[8,64,128]{2,1,0:T(8,128)S(1)} %get-tuple-element.35), channel_id=1, replica_groups=mesh['sample'=8,'slab'=64] {'sample'}, dimensions={0} | all-to-all | bytes 524288 | tf_op jit(solution)/shard_map/all_to_all | solution.py:461
  61.5 0.6 multiply_bitcast_fusion
  (1 shorter events, 0.0 us)
Async XLA Ops:
  0.6 38.9 %copy-start = (s32[1,4,64,128]{3,2,1,0:T(8,128)S(1)}, s32[1,4,64,128]{3,2,1,0:T(8,128)}, u32[]{:S(2)}) copy-start(s32[1,4,64,128]{3,2,1,0:T(8,128)} %region.3) | copy-start | bytes 393220
  2.6 22.0 %collective-permute-start = (f32[5,64,128]{2,1,0:T(8,128)S(1)}, f32[5,64,128]{2,1,0:T(8,128)S(1)}, u32[]{:S(2)}, u32[]{:S(2)}) collective-permute-start(f32[5,64,128]{2,1,0:T(8,128)S(1)} %get-tuple-element.24), channel_id=1, source_target_pairs={{0,63},{1,2},{2,1},{3,4},{4,3},{5,6},{6,5},{7,8},{8,7},{9,10},{10,... | collective-permute-start | bytes 491528 | tf_op jit(solution)/shard_map/ppermute | solution.py:412
  19.1 6.6 %collective-permute-start.1 = (f32[5,64,128]{2,1,0:T(8,128)S(1)}, f32[5,64,128]{2,1,0:T(8,128)S(1)}, u32[]{:S(2)}, u32[]{:S(2)}) collective-permute-start(f32[5,64,128]{2,1,0:T(8,128)S(1)} %get-tuple-element.25), channel_id=1, source_target_pairs={{0,1},{1,0},{2,3},{3,2},{4,5},{5,4},{6,7},{7,6},{8,9},{9,8},{10,11... | collective-permute-start | bytes 491528 | tf_op jit(solution)/shard_map/ppermute | solution.py:412
  26.4 16.0 %collective-permute-start.2 = (f32[5,64,128]{2,1,0:T(8,128)S(1)}, f32[5,64,128]{2,1,0:T(8,128)S(1)}, u32[]{:S(2)}, u32[]{:S(2)}) collective-permute-start(f32[5,64,128]{2,1,0:T(8,128)S(1)} %get-tuple-element.31), channel_id=1, source_target_pairs={{0,63},{1,2},{2,1},{3,4},{4,3},{5,6},{6,5},{7,8},{8,7},{9,10},{10,... | collective-permute-start | bytes 491528 | tf_op jit(solution)/shard_map/ppermute | solution.py:412
  37.6 6.1 %collective-permute-start.3 = (f32[5,64,128]{2,1,0:T(8,128)S(1)}, f32[5,64,128]{2,1,0:T(8,128)S(1)}, u32[]{:S(2)}, u32[]{:S(2)}) collective-permute-start(f32[5,64,128]{2,1,0:T(8,128)S(1)} %get-tuple-element.32), channel_id=1, source_target_pairs={{0,1},{1,0},{2,3},{3,2},{4,5},{5,4},{6,7},{7,6},{8,9},{9,8},{10,11... | collective-permute-start | bytes 491528 | tf_op jit(solution)/shard_map/ppermute | solution.py:412

commit v2 on v1

--- a/solution.py
+++ b/solution.py
@@ -203,8 +203,8 @@
     s2[...] = s_v[1]
 
 
-def first_inside(dev, solid, inner, edge, sums, field, dev_v, f_v, g_v, sems_in, sems_out):
-    into, out = Copies(sems_in), Copies(sems_out)
+def first_inside(dev, solid, inner, edge, sums, g_v, dev_v, f_v, sems):
+    into = Copies(sems)
     into.start(dev.at[0, :, pl.ds(1, 2)], dev_v)
     into.finish()
     for side in range(2):
@@ -222,19 +222,11 @@
             source[q] = (inner, (side, j))
         dest = [(g_v, (q, side + 1 + MOVES[q][2])) for q in range(19)]
         collide_plane(rows_from(source), rows_of(solid, (side + 1,)), dest)
-    for low, count in FLAT_RUNS:
-        run = pl.ds(low, count)
-        out.start(g_v.at[run, pl.ds(1, 2)], field.at[0, run, pl.ds(1, 2)])
-    for q in DOWN:
-        out.start(g_v.at[q, pl.ds(0, 2)], field.at[0, q, pl.ds(0, 2)])
-    for q in UP:
-        out.start(g_v.at[q, pl.ds(2, 2)], field.at[0, q, pl.ds(2, 2)])
     for z, have in enumerate((DOWN, FLAT + DOWN, FLAT + UP, UP)):
         for turn in range(NY // STEP):
             rows = pl.ds(STEP * turn, STEP)
             for k, value in enumerate(sums_of({q: g_v[q, z, rows] for q in have})):
                 sums[z, k, rows] = value
-    out.finish()
 
 
 def second_edges(solid, flat, edge, r1, r2, s1, s2, flat2, inner2, s_v):
@@ -316,9 +308,15 @@
     lax.fori_loop(0, first.shape[0] // rows, body, 0)
 
 
-def inside_regions(solid, region, sums, flat2, inner2, held, table, part, field, first_v, frac_v, sems):
-    del held
+def inside_regions(solid, region, sums, flat2, inner2, g_v, table, part, field, first_v, frac_v, sems):
     out = Copies(sems)
+    for low, count in FLAT_RUNS:
+        run = pl.ds(low, count)
+        out.start(g_v.at[run, pl.ds(1, 2)], field.at[0, run, pl.ds(1, 2)])
+    for q in DOWN:
+        out.start(g_v.at[q, pl.ds(0, 2)], field.at[0, q, pl.ds(0, 2)])
+    for q in UP:
+        out.start(g_v.at[q, pl.ds(2, 2)], field.at[0, q, pl.ds(2, 2)])
     for side, z in EDGES:
         for j, (low, count) in ((0, FLAT_RUNS[0]), (FLAT_RUNS[0][1], FLAT_RUNS[1])):
             out.start(flat2.at[side, pl.ds(j, count)], field.at[0, pl.ds(low, count), z])
@@ -423,12 +421,12 @@
         kinds=(i32, F32, F32, F32, F32),
     )(deviation, solid)
     r1, r2 = exchange(s1, s2)
-    edge, sums, field = call(
+    edge, sums, moved = call(
         first_inside,
-        "HVVVVH",
-        [(2,) + five, (CZ, 4) + plane, whole],
-        [((19, 2) + plane, BF16), ((2, 19) + plane, F32), ((19, CZ) + plane, F32)],
-        (1, 12),
+        "HVVVVV",
+        [(2,) + five, (CZ, 4) + plane, (19, CZ) + plane],
+        [((19, 2) + plane, BF16), ((2, 19) + plane, F32)],
+        (1,),
         20000000,
     )(deviation, rock, inner)
     s1, s2, flat, inner = call(
@@ -442,13 +440,12 @@
     r1, r2 = exchange(s1, s2)
     table, part, field = call(
         inside_regions,
-        "VVVVVHVVH",
+        "VVVVVVVVH",
         [(256, 256), (2, 4) + plane, whole],
         [(rows, F32), (rows, F32)],
-        (14,),
+        (26,),
         2000000000,
-        {5: 2},
-    )(rock, region, sums, flat, inner, field)
+    )(rock, region, sums, flat, inner, moved)
     chunks, field = call(
         edge_regions,
         "VVVVVVHVH",

time: 62.5 us -> 62.5 us (level)
  Pallas kernels: 11.6 us -> 10.6 us
  waiting for transfers between devices: 2.49 us -> 3.47 us
    pallas_call x2, Pallas kernels: 6.32 us -> 5.34 us  [the longest x1 3 us: per_device(): call(inside_regions, 'VVVVVVVVH', [(256, 256), (2, 4) + plane, whole], [(...]
  transfers between devices with their start and end apart: 4 -> 4, of which waited for: 2 -> 3; matrix products, arithmetic and copies ran while one was open for 0% -> 0% of each run, Pallas kernels for 10% -> 9%
where the time goes in v2:
time: 62.5 us; the launch traced here: 62.2 us
  starting transfers between devices  31.6 us (51%)
  blocking collectives  15.1 us (24%)
  Pallas kernels  10.6 us (17%)
  waiting for transfers between devices  3.47 us (6%)
  between operations  0.72 us (1%)
  other arithmetic  0.64 us (1%)
    ppermute x2, starting transfers between devices, exchange(): lax.ppermute(first, 'slab', far)  27.8 us
    all_to_all x1, blocking collectives, per_device(): chunks = lax.all_to_all(chunks, 'sample', 0, 0)  15.1 us
    ppermute x2, starting transfers between devices, exchange(): lax.ppermute(second, 'slab', near)  3.84 us
    pallas_call x1, Pallas kernels, per_device(): call(inside_regions, 'VVVVVVVVH', [(256, 256), (2, 4) + plane, whole], [(...  3 us
    ppermute x2, waiting for transfers between devices, exchange(): lax.ppermute(second, 'slab', near)  2.96 us
    pallas_call x1, Pallas kernels, per_device(): call(edge_regions, 'VVVVVVHVH', [(8, LEVELS, NX), whole], [(rows, F32), (...  2.8 us
    pallas_call x1, Pallas kernels, per_device(): call(first_inside, 'HVVVVV', [(2,) + five, (CZ, 4) + plane, (19, CZ) + pl...  2.34 us
    pallas_call x1, Pallas kernels, per_device(): call(first_edges, 'HHVVVVV', [(CZ,) + plane, five, five, (2,) + nine, (2,...  1.91 us
  transfers between devices with their start and end apart: 4, of which 3 were waited for; matrix products, arithmetic and copies ran while one was open for 0% of the time, Pallas kernels for 9%

profile of v2, /device:TPU:1, one launch (start us, length us, event | category | flops | bytes accessed | tf_op | source)
XLA Modules:
  0.0 62.2 jit_solution(14100993888097888861)
XLA Ops:
  0.6 0.0 copy-start
  0.6 1.9 %first_edges.1 = (s32[4,64,128]{2,1,0:T(8,128)S(1)}, f32[5,64,128]{2,1,0:T(8,128)S(1)}, f32[5,64,128]{2,1,0:T(8,128)S(1)}, f32[2,9,64,128]{3,2,1,0:T(8,128)S(1)}, f32[2,5,64,128]{3,2,1,0:T(8,128)S(1)}) custom-call(bf16[1,19,4,64,128]{4,3,2,1,0:T(8,128)(2,1)} %dev.3, s32[1,4,64,128]{3,2,1,0:T(8,128)} %solid.1), custom_call_target="tpu_custom_call" | custom-call | flops 10000000 | bytes 4000000 | tf_op jit(solution)/shard_map/first_edges/pallas_call | solution.py:414
  2.6 16.6 %collective-permute-start = (f32[5,64,128]{2,1,0:T(8,128)S(1)}, f32[5,64,128]{2,1,0:T(8,128)S(1)}, u32[]{:S(2)}, u32[]{:S(2)}) collective-permute-start(f32[5,64,128]{2,1,0:T(8,128)S(1)} %get-tuple-element.24), channel_id=1, source_target_pairs={{0,63},{1,2},{2,1},{3,4},{4,3},{5,6},{6,5},{7,8},{8,7},{9,10},{10,... | collective-permute-start | bytes 491528 | tf_op jit(solution)/shard_map/ppermute | solution.py:410
  19.1 1.9 %collective-permute-start.1 = (f32[5,64,128]{2,1,0:T(8,128)S(1)}, f32[5,64,128]{2,1,0:T(8,128)S(1)}, u32[]{:S(2)}, u32[]{:S(2)}) collective-permute-start(f32[5,64,128]{2,1,0:T(8,128)S(1)} %get-tuple-element.25), channel_id=1, source_target_pairs={{0,1},{1,0},{2,3},{3,2},{4,5},{5,4},{6,7},{7,6},{8,9},{9,8},{10,11... | collective-permute-start | bytes 491528 | tf_op jit(solution)/shard_map/ppermute | solution.py:410
  21.1 2.3 %first_inside.1 = (f32[2,5,64,128]{3,2,1,0:T(8,128)S(1)}, f32[4,4,64,128]{3,2,1,0:T(8,128)S(1)}, f32[19,4,64,128]{3,2,1,0:T(8,128)S(1)}) custom-call(bf16[1,19,4,64,128]{4,3,2,1,0:T(8,128)(2,1)} %dev.3, s32[4,64,128]{2,1,0:T(8,128)S(1)} %get-tuple-element.19.solid, f32[2,5,64,128]{3,2,1,0:T(8,128)S(1)} %get-tuple-element.20.inner), custom_call_target="tpu_custom_call" | custom-call | flops 20000000 | bytes 4000000 | tf_op jit(solution)/shard_map/first_inside/pallas_call | solution.py:424
  23.4 0.5 collective-permute-done.r1
  23.9 1.9 %collective-permute-done.1.r2 = f32[5,64,128]{2,1,0:T(8,128)S(1)} collective-permute-done((f32[5,64,128]{2,1,0:T(8,128)S(1)}, f32[5,64,128]{2,1,0:T(8,128)S(1)}, u32[]{:S(2)}, u32[]{:S(2)}) %collective-permute-start.1) | collective-permute-done | bytes 163872 | tf_op jit(solution)/shard_map/ppermute | solution.py:410
  25.8 0.6 second_edges.1
  26.4 11.2 %collective-permute-start.2 = (f32[5,64,128]{2,1,0:T(8,128)S(1)}, f32[5,64,128]{2,1,0:T(8,128)S(1)}, u32[]{:S(2)}, u32[]{:S(2)}) collective-permute-start(f32[5,64,128]{2,1,0:T(8,128)S(1)} %get-tuple-element.31), channel_id=1, source_target_pairs={{0,63},{1,2},{2,1},{3,4},{4,3},{5,6},{6,5},{7,8},{8,7},{9,10},{10,... | collective-permute-start | bytes 491528 | tf_op jit(solution)/shard_map/ppermute | solution.py:410
  37.6 1.9 %collective-permute-start.3 = (f32[5,64,128]{2,1,0:T(8,128)S(1)}, f32[5,64,128]{2,1,0:T(8,128)S(1)}, u32[]{:S(2)}, u32[]{:S(2)}) collective-permute-start(f32[5,64,128]{2,1,0:T(8,128)S(1)} %get-tuple-element.32), channel_id=1, source_target_pairs={{0,1},{1,0},{2,3},{3,2},{4,5},{5,4},{6,7},{7,6},{8,9},{9,8},{10,11... | collective-permute-start | bytes 491528 | tf_op jit(solution)/shard_map/ppermute | solution.py:410
  39.5 0.0 copy-done
  39.5 3.0 %inside_regions.1 = (f32[256,256]{1,0:T(8,128)S(1)}, f32[2,4,64,128]{3,2,1,0:T(8,128)S(1)}, f32[1,19,4,64,128]{4,3,2,1,0:T(8,128)}) custom-call(s32[4,64,128]{2,1,0:T(8,128)S(1)} %get-tuple-element.19.solid, s32[1,4,64,128]{3,2,1,0:T(8,128)S(1)} %copy-done, f32[4,4,64,128]{3,2,1,0:T(8,128)S(1)} %get-tuple-element.21.sums, ...), custom_call_target="tpu_custom_call" | custom-call | flops 2000000000 | bytes 4000000 | tf_op jit(solution)/shard_map/inside_regions/pallas_call | solution.py:441
  42.5 0.0 collective-permute-done.2.r1
  42.5 1.1 %collective-permute-done.3.r2 = f32[5,64,128]{2,1,0:T(8,128)S(1)} collective-permute-done((f32[5,64,128]{2,1,0:T(8,128)S(1)}, f32[5,64,128]{2,1,0:T(8,128)S(1)}, u32[]{:S(2)}, u32[]{:S(2)}) %collective-permute-start.3) | collective-permute-done | bytes 163872 | tf_op jit(solution)/shard_map/ppermute | solution.py:410
  43.6 2.8 %edge_regions.1 = (f32[8,64,128]{2,1,0:T(8,128)S(1)}, f32[1,19,4,64,128]{4,3,2,1,0:T(8,128)}) custom-call(s32[4,64,128]{2,1,0:T(8,128)S(1)} %get-tuple-element.19.solid, s32[1,4,64,128]{3,2,1,0:T(8,128)S(1)} %copy-done, f32[256,256]{1,0:T(8,128)S(1)} %get-tuple-element.29.table, ...), custom_call_target="tpu_custom_call", output_to_operand_aliasing={{1}: (6, {})} | custom-call | flops 2000000000 | bytes 4000000 | tf_op jit(solution)/shard_map/edge_regions/pallas_call | solution.py:449
  46.4 15.1 %all_to_all.5 = f32[8,64,128]{2,1,0:T(8,128)S(1)} all-to-all(f32[8,64,128]{2,1,0:T(8,128)S(1)} %get-tuple-element.35), channel_id=1, replica_groups=mesh['sample'=8,'slab'=64] {'sample'}, dimensions={0} | all-to-all | bytes 524288 | tf_op jit(solution)/shard_map/all_to_all | solution.py:458
  61.5 0.6 multiply_bitcast_fusion
  (1 shorter events, 0.0 us)
Async XLA Ops:
  0.6 38.9 %copy-start = (s32[1,4,64,128]{3,2,1,0:T(8,128)S(1)}, s32[1,4,64,128]{3,2,1,0:T(8,128)}, u32[]{:S(2)}) copy-start(s32[1,4,64,128]{3,2,1,0:T(8,128)} %region.3) | copy-start | bytes 393220
  2.6 21.4 %collective-permute-start = (f32[5,64,128]{2,1,0:T(8,128)S(1)}, f32[5,64,128]{2,1,0:T(8,128)S(1)}, u32[]{:S(2)}, u32[]{:S(2)}) collective-permute-start(f32[5,64,128]{2,1,0:T(8,128)S(1)} %get-tuple-element.24), channel_id=1, source_target_pairs={{0,63},{1,2},{2,1},{3,4},{4,3},{5,6},{6,5},{7,8},{8,7},{9,10},{10,... | collective-permute-start | bytes 491528 | tf_op jit(solution)/shard_map/ppermute | solution.py:410
  19.1 6.6 %collective-permute-start.1 = (f32[5,64,128]{2,1,0:T(8,128)S(1)}, f32[5,64,128]{2,1,0:T(8,128)S(1)}, u32[]{:S(2)}, u32[]{:S(2)}) collective-permute-start(f32[5,64,128]{2,1,0:T(8,128)S(1)} %get-tuple-element.25), channel_id=1, source_target_pairs={{0,1},{1,0},{2,3},{3,2},{4,5},{5,4},{6,7},{7,6},{8,9},{9,8},{10,11... | collective-permute-start | bytes 491528 | tf_op jit(solution)/shard_map/ppermute | solution.py:410
  26.4 16.2 %collective-permute-start.2 = (f32[5,64,128]{2,1,0:T(8,128)S(1)}, f32[5,64,128]{2,1,0:T(8,128)S(1)}, u32[]{:S(2)}, u32[]{:S(2)}) collective-permute-start(f32[5,64,128]{2,1,0:T(8,128)S(1)} %get-tuple-element.31), channel_id=1, source_target_pairs={{0,63},{1,2},{2,1},{3,4},{4,3},{5,6},{6,5},{7,8},{8,7},{9,10},{10,... | collective-permute-start | bytes 491528 | tf_op jit(solution)/shard_map/ppermute | solution.py:410
  37.6 6.1 %collective-permute-start.3 = (f32[5,64,128]{2,1,0:T(8,128)S(1)}, f32[5,64,128]{2,1,0:T(8,128)S(1)}, u32[]{:S(2)}, u32[]{:S(2)}) collective-permute-start(f32[5,64,128]{2,1,0:T(8,128)S(1)} %get-tuple-element.32), channel_id=1, source_target_pairs={{0,1},{1,0},{2,3},{3,2},{4,5},{5,4},{6,7},{7,6},{8,9},{9,8},{10,11... | collective-permute-start | bytes 491528 | tf_op jit(solution)/shard_map/ppermute | solution.py:410
